TPU v7x, 32 devices: a whole 2x2x4 slice. The times are simulated.
32 devices in a mesh: dp: 16 (over z, y, core), tensor: 2 (over x).
Axes of the slice: x: 2, y: 2, z: 4, core: 2. Of those that a mesh axis runs over, the one named last changes fastest.
Arguments:
- tokens: bfloat16 [24576, 640], P('dp'), may hold values from -6 to 6
- w_query: bfloat16 [640, 1024], P(None, 'tensor'), may hold values from -0.25 to 0.25
- w_key: bfloat16 [640, 256], replicated, may hold values from -0.25 to 0.25
- w_value: bfloat16 [640, 256], replicated, may hold values from -0.25 to 0.25
- w_output: bfloat16 [1024, 640], P('tensor'), may hold values from -0.1875 to 0.1875
- w_gate: bfloat16 [640, 2048], P(None, 'tensor'), may hold values from -0.25 to 0.25
- w_up: bfloat16 [640, 2048], P(None, 'tensor'), may hold values from -0.25 to 0.25
- w_down: bfloat16 [2048, 640], P('tensor'), may hold values from -0.125 to 0.125
- gain_input: float32 [640], replicated, may hold values from -0.4 to 0.6
- gain_query: float32 [256], replicated, may hold values from -0.4 to 0.6
- gain_key: float32 [256], replicated, may hold values from -0.4 to 0.6
- gain_post_attn: float32 [640], replicated, may hold values from -0.4 to 0.6
- gain_pre_ffn: float32 [640], replicated, may hold values from -0.4 to 0.6
- gain_post_ffn: float32 [640], replicated, may hold values from -0.4 to 0.6
- out_grad: bfloat16 [24576, 640], P('dp'), may hold values from -6 to 6
- lengths: int32 [24], replicated, may hold values from 1 to 1536, as said below
- holder: int32 [24], replicated, may hold values from 0 to 15
Outputs:
- layer_out: float32 [24576, 640], P('dp')
- tokens_grad: float32 [24576, 640], P('dp')
- grad_w_query: float32 [640, 1024], P(None, 'tensor')
- grad_w_key: float32 [640, 256], replicated
- grad_w_value: float32 [640, 256], replicated
- grad_w_output: float32 [1024, 640], P('tensor')
- grad_w_gate: float32 [640, 2048], P(None, 'tensor')
- grad_w_up: float32 [640, 2048], P(None, 'tensor')
- grad_w_down: float32 [2048, 640], P('tensor')
- grad_gain_input: float32 [640], replicated
- grad_gain_query: float32 [256], replicated
- grad_gain_key: float32 [256], replicated
- grad_gain_post_attn: float32 [640], replicated
- grad_gain_pre_ffn: float32 [640], replicated
- grad_gain_post_ffn: float32 [640], replicated
Inputs may be any that keep to these rules, and one draw needn't show every extreme that they name: The sequences of one index d of dp (holder = d) have lengths summing to at most 1536; one sequence has exactly 1536 tokens; an index of dp holds 0 to 3 sequences.
All inputs are finite; a program needn't handle non-finite values.
Results may differ from a plain program's by a relative error of at most 0.015.
Values sent between devices are 32-bit elements; how exact they have to be, the bound alone decides.
A program may use at most 192 MiB of HBM per device.

v0:
```python
import jax
import jax.numpy as jnp
from jax import lax
from jax.sharding import PartitionSpec as P

HD = 256
EPS = 1e-06
THETA = 1000000.0


def layout(lengths, holder, device, tok_rows):
    seq_count = lengths.shape[0]
    owned_mask = holder == device
    local_len = jnp.where(owned_mask, lengths, 0)
    starts = jnp.cumsum(local_len) - local_len
    row_ids = jnp.arange(tok_rows, dtype=jnp.int32)[:, None]
    inside = (
        owned_mask[None, :]
        & (row_ids >= starts[None, :])
        & (row_ids < (starts + local_len)[None, :])
    )
    inside_int = inside.astype(jnp.int32)
    segment = (
        jnp.sum(inside_int * (jnp.arange(seq_count, dtype=jnp.int32)[None, :] + 1), axis=1) - 1
    )
    position = jnp.sum(inside_int * (row_ids - starts[None, :]), axis=1)
    return (segment, position)


def rotary_tables(position):
    half_width = HD // 2
    frequency = THETA ** (-(2.0 * jnp.arange(half_width, dtype=jnp.float32)) / HD)
    angles = position.astype(jnp.float32)[:, None] * frequency[None, :]
    angles = jnp.concatenate([angles, angles], axis=1)
    return (jnp.cos(angles), jnp.sin(angles))


def rotate(vectors, cosine, sine):
    half_width = vectors.shape[-1] // 2
    turned = jnp.concatenate([-vectors[..., half_width:], vectors[..., :half_width]], axis=-1)
    return vectors * cosine + turned * sine


def unrotate(grads_in, cosine, sine):
    half_width = grads_in.shape[-1] // 2
    weighted = grads_in * sine
    turned = jnp.concatenate([weighted[..., half_width:], -weighted[..., :half_width]], axis=-1)
    return grads_in * cosine + turned


def norm_forward(vectors, scaling):
    inverse = lax.rsqrt(jnp.mean(vectors * vectors, axis=-1, keepdims=True) + EPS)
    plain = vectors * inverse
    return (plain * (1.0 + scaling), plain, inverse)


def norm_backward(grads_in, plain, inverse, scaling):
    scaled = grads_in * (1.0 + scaling)
    grads_out = inverse * (scaled - plain * jnp.mean(scaled * plain, axis=-1, keepdims=True))
    gain_grad = jnp.sum(grads_in * plain, axis=tuple(range(grads_in.ndim - 1)))
    return (grads_out, gain_grad)


def left_dot(first, second):
    return lax.dot_general(
        first, second, (((0,), (0,)), ((), ())), preferred_element_type=jnp.float32
    )


def right_dot(first, second):
    return lax.dot_general(
        first, second, (((1,), (1,)), ((), ())), preferred_element_type=jnp.float32
    )


def left_full(first, second):
    return lax.dot_general(
        first,
        second,
        (((0,), (0,)), ((), ())),
        precision=lax.Precision.HIGHEST,
        preferred_element_type=jnp.float32,
    )


def right_full(first, second):
    return lax.dot_general(
        first,
        second,
        (((1,), (1,)), ((), ())),
        precision=lax.Precision.HIGHEST,
        preferred_element_type=jnp.float32,
    )


def gelu_tanh(vectors):
    return jax.nn.gelu(vectors, approximate=True)


def block_scores(query_block, key_states, segment, first_row, score_scale):
    block_rows = query_block.shape[0]
    total_rows = key_states.shape[0]
    row_ids = first_row + jnp.arange(block_rows, dtype=jnp.int32)
    column_ids = jnp.arange(total_rows, dtype=jnp.int32)
    seg_rows = lax.dynamic_slice_in_dim(segment, first_row, block_rows)
    allowed = (seg_rows[:, None] == segment[None, :]) & (seg_rows[:, None] >= 0) & (
        column_ids[None, :] <= row_ids[:, None]
    ) | (column_ids[None, :] == row_ids[:, None])
    raw_scores = (
        jnp.einsum("qhd,kd->hqk", query_block, key_states, preferred_element_type=jnp.float32)
        * score_scale
    )
    return jnp.where(allowed[None, :, :], raw_scores, -1e30)


def local(
    tokens,
    w_query,
    w_key,
    w_value,
    w_output,
    w_gate,
    w_up,
    w_down,
    gain_input,
    gain_query,
    gain_key,
    gain_post_attn,
    gain_pre_ffn,
    gain_post_ffn,
    out_grad,
    lengths,
    holder,
):
    tok_rows = tokens.shape[0]
    local_heads = w_query.shape[1] // HD
    score_scale = HD ** (-0.5)
    device = lax.axis_index("dp")
    segment, position = layout(lengths, holder, device, tok_rows)
    cosine, sine = rotary_tables(position)
    block_rows = min(512, tok_rows)
    block_count = tok_rows // block_rows
    first_rows = jnp.arange(block_count, dtype=jnp.int32) * block_rows
    source = tokens.astype(jnp.float32)
    normed, normed_plain, normed_inverse = norm_forward(source, gain_input)
    normed_low = normed.astype(jnp.bfloat16)
    query_pre = jnp.dot(normed_low, w_query, preferred_element_type=jnp.float32).reshape(
        tok_rows, local_heads, HD
    )
    key_pre = jnp.dot(normed_low, w_key, preferred_element_type=jnp.float32)
    value_pre = jnp.dot(normed_low, w_value, preferred_element_type=jnp.float32)
    query_normed, query_plain, query_inverse = norm_forward(query_pre, gain_query)
    query_states = rotate(query_normed, cosine[:, None, :], sine[:, None, :]).astype(jnp.bfloat16)
    key_normed, key_plain, key_inverse = norm_forward(key_pre, gain_key)
    key_states = rotate(key_normed, cosine, sine).astype(jnp.bfloat16)
    value_states = value_pre.astype(jnp.bfloat16)
    query_blocks = query_states.reshape(block_count, block_rows, local_heads, HD)

    def forward_block(inputs):
        query_block, first_row = inputs
        scores = block_scores(query_block, key_states, segment, first_row, score_scale)
        row_max = jnp.max(scores, axis=-1, keepdims=True)
        exponent = jnp.exp(scores - row_max)
        row_total = jnp.sum(exponent, axis=-1, keepdims=True)
        attn_probs = exponent / row_total
        mixed_block = jnp.einsum(
            "hqk,kd->qhd",
            attn_probs.astype(jnp.bfloat16),
            value_states,
            preferred_element_type=jnp.float32,
        )
        return (mixed_block, (row_max + jnp.log(row_total))[..., 0])

    mixed_blocks, log_totals = lax.map(forward_block, (query_blocks, first_rows))
    mixed_heads = mixed_blocks.reshape(tok_rows, local_heads * HD).astype(jnp.bfloat16)
    branch = lax.psum(jnp.dot(mixed_heads, w_output, preferred_element_type=jnp.float32), "tensor")
    post_attn, post_attn_plain, post_attn_inverse = norm_forward(branch, gain_post_attn)
    middle = source + post_attn
    normed2, normed2_plain, normed2_inverse = norm_forward(middle, gain_pre_ffn)
    normed2_low = normed2.astype(jnp.bfloat16)
    gate_proj = jnp.dot(normed2_low, w_gate, preferred_element_type=jnp.float32)
    up_proj = jnp.dot(normed2_low, w_up, preferred_element_type=jnp.float32)
    activation, gelu_pull = jax.vjp(gelu_tanh, gate_proj)
    hidden = (activation * up_proj).astype(jnp.bfloat16)
    ffn_sum = lax.psum(jnp.dot(hidden, w_down, preferred_element_type=jnp.float32), "tensor")
    post_ffn, post_ffn_plain, post_ffn_inverse = norm_forward(ffn_sum, gain_post_ffn)
    layer_out = middle + post_ffn
    valid = (segment >= 0).astype(jnp.float32)[:, None]
    upstream = out_grad.astype(jnp.float32) * valid
    grad_ffn, grad_post_ffn = norm_backward(
        upstream, post_ffn_plain, post_ffn_inverse, gain_post_ffn
    )
    grad_ffn_low = grad_ffn.astype(jnp.bfloat16)
    grad_down = left_dot(hidden, grad_ffn_low)
    grad_hidden = right_dot(grad_ffn_low, w_down)
    grad_gate_low = gelu_pull(grad_hidden * up_proj)[0].astype(jnp.bfloat16)
    grad_up_low = (grad_hidden * activation).astype(jnp.bfloat16)
    grad_gate = left_dot(normed2_low, grad_gate_low)
    grad_up = left_dot(normed2_low, grad_up_low)
    grad_normed2 = lax.psum(
        right_dot(grad_gate_low, w_gate) + right_dot(grad_up_low, w_up), "tensor"
    )
    grad_pre_part, grad_pre_ffn = norm_backward(
        grad_normed2, normed2_plain, normed2_inverse, gain_pre_ffn
    )
    grad_middle = upstream + grad_pre_part
    grad_branch, grad_post_attn = norm_backward(
        grad_middle, post_attn_plain, post_attn_inverse, gain_post_attn
    )
    grad_branch_low = grad_branch.astype(jnp.bfloat16)
    grad_output = left_dot(mixed_heads, grad_branch_low)
    grad_mixed = (
        right_dot(grad_branch_low, w_output)
        .astype(jnp.bfloat16)
        .reshape(block_count, block_rows, local_heads, HD)
    )

    def backward_block(sums_carry, inputs):
        key_sum, value_sum = sums_carry
        query_block, mixed_grad_block, total_block, first_row = inputs
        scores = block_scores(query_block, key_states, segment, first_row, score_scale)
        attn_probs = jnp.exp(scores - total_block[..., None])
        grad_probs = jnp.einsum(
            "qhd,kd->hqk", mixed_grad_block, value_states, preferred_element_type=jnp.float32
        )
        grad_scores = (
            attn_probs
            * (grad_probs - jnp.sum(attn_probs * grad_probs, axis=-1, keepdims=True))
            * score_scale
        ).astype(jnp.bfloat16)
        query_grad_block = jnp.einsum(
            "hqk,kd->qhd", grad_scores, key_states, preferred_element_type=jnp.float32
        )
        key_sum = key_sum + jnp.einsum(
            "hqk,qhd->kd", grad_scores, query_block, preferred_element_type=jnp.float32
        )
        value_sum = value_sum + jnp.einsum(
            "hqk,qhd->kd",
            attn_probs.astype(jnp.bfloat16),
            mixed_grad_block,
            preferred_element_type=jnp.float32,
        )
        return ((key_sum, value_sum), query_grad_block)

    zeroes = jnp.zeros((tok_rows, HD), jnp.float32)
    (grad_keys_part, grad_values_part), query_grad_blocks = lax.scan(
        backward_block, (zeroes, zeroes), (query_blocks, grad_mixed, log_totals, first_rows)
    )
    grad_queries = query_grad_blocks.reshape(tok_rows, local_heads, HD)
    grad_query_pre, grad_gain_query_part = norm_backward(
        unrotate(grad_queries, cosine[:, None, :], sine[:, None, :]),
        query_plain,
        query_inverse,
        gain_query,
    )
    grad_query_low = grad_query_pre.astype(jnp.bfloat16).reshape(tok_rows, local_heads * HD)
    grad_query = left_dot(normed_low, grad_query_low)
    normed_wide = normed_low.astype(jnp.float32)
    w_key_wide = w_key.astype(jnp.float32)
    w_value_wide = w_value.astype(jnp.float32)
    grad_keys, grad_values, from_query, grad_gain_query = lax.psum(
        (
            grad_keys_part,
            grad_values_part,
            right_dot(grad_query_low, w_query),
            grad_gain_query_part,
        ),
        "tensor",
    )
    grad_key_pre, grad_gain_key_local = norm_backward(
        unrotate(grad_keys, cosine, sine), key_plain, key_inverse, gain_key
    )
    grad_key_local = left_full(normed_wide, grad_key_pre)
    grad_value_local = left_full(normed_wide, grad_values)
    grad_normed = (
        from_query + right_full(grad_key_pre, w_key_wide) + right_full(grad_values, w_value_wide)
    )
    grad_key, grad_value, grad_gain_key = lax.psum(
        (grad_key_local, grad_value_local, grad_gain_key_local), "dp"
    )
    grad_input_part, grad_gain_input = norm_backward(
        grad_normed, normed_plain, normed_inverse, gain_input
    )
    tokens_grad = grad_middle + grad_input_part
    all_summed = (
        lax.psum_scatter(grad_query, "dp", scatter_dimension=0, tiled=True),
        lax.psum_scatter(grad_output, "dp", scatter_dimension=0, tiled=True),
        lax.psum_scatter(grad_gate, "dp", scatter_dimension=0, tiled=True),
        lax.psum_scatter(grad_up, "dp", scatter_dimension=0, tiled=True),
        lax.psum_scatter(grad_down, "dp", scatter_dimension=0, tiled=True),
        lax.psum_scatter(grad_gain_input, "dp", scatter_dimension=0, tiled=True),
        lax.psum_scatter(grad_gain_query, "dp", scatter_dimension=0, tiled=True),
        lax.psum_scatter(grad_post_attn, "dp", scatter_dimension=0, tiled=True),
        lax.psum_scatter(grad_pre_ffn, "dp", scatter_dimension=0, tiled=True),
        lax.psum_scatter(grad_post_ffn, "dp", scatter_dimension=0, tiled=True),
    )
    all_full = (
        lax.all_gather(all_summed[0], "dp", axis=0, tiled=True),
        lax.all_gather(all_summed[1], "dp", axis=0, tiled=True),
        lax.all_gather(all_summed[2], "dp", axis=0, tiled=True),
        lax.all_gather(all_summed[3], "dp", axis=0, tiled=True),
        lax.all_gather(all_summed[4], "dp", axis=0, tiled=True),
        lax.all_gather(all_summed[5], "dp", axis=0, tiled=True),
        lax.all_gather(all_summed[6], "dp", axis=0, tiled=True),
        lax.all_gather(all_summed[7], "dp", axis=0, tiled=True),
        lax.all_gather(all_summed[8], "dp", axis=0, tiled=True),
        lax.all_gather(all_summed[9], "dp", axis=0, tiled=True),
    )
    return (
        layer_out,
        tokens_grad,
        all_full[0],
        grad_key,
        grad_value,
        all_full[1],
        all_full[2],
        all_full[3],
        all_full[4],
        all_full[5],
        all_full[6],
        grad_gain_key,
        all_full[7],
        all_full[8],
        all_full[9],
    )


def solution(mesh):
    return jax.shard_map(
        local,
        mesh=mesh,
        in_specs=(
            P("dp", None),
            P(None, "tensor"),
            P(),
            P(),
            P("tensor", None),
            P(None, "tensor"),
            P(None, "tensor"),
            P("tensor", None),
            P(),
            P(),
            P(),
            P(),
            P(),
            P(),
            P("dp", None),
            P(),
            P(),
        ),
        out_specs=(
            P("dp", None),
            P("dp", None),
            P(None, "tensor"),
            P(),
            P(),
            P("tensor", None),
            P(None, "tensor"),
            P(None, "tensor"),
            P("tensor", None),
            P(),
            P(),
            P(),
            P(),
            P(),
            P(),
        ),
        check_vma=False,
    )
```

profile of v0, /device:TPU:0, one launch (start us, length us, event | category | flops | bytes accessed | tf_op | source)
XLA Modules:
  0.0 1547.5 jit_solution(16992179626408646211)
XLA Ops:
  69.3 39.3 %while.29 = (s32[]{:T(128)}, bf16[3,512,2,256]{3,1,2,0:T(8,128)(2,1)}, f32[3,2,512]{2,1,0:T(2,128)S(1)}, s32[3]{0:T(128)S(1)}, s32[1536]{0:T(1024)S(1)}, /*index...) while((s32[]{:T(128)}, ...), condition=%wide.region_9.10_spmd.clone, body=%wide.region_6.9_spmd.sunk.clone | while | flops 1634205696 | bytes 40944880 | solution.py:174
  117.3 105.1 %all-reduce.20.cloned.1.call-done = f32[1536,640]{1,0:T(8,128)} async-done(((f32[1536,640]{1,0:T(8,128)}), f32[1536,640]{1,0:T(8,128)}) %all-reduce.20.cloned.1.call-update) | async-done | bytes 3932176 | tf_op jit(solution)/shard_map/psum | solution.py:176
  244.9 102.4 %all-reduce.22.cloned.1.call-done = f32[1536,640]{1,0:T(8,128)} async-done(((f32[1536,640]{1,0:T(8,128)}), f32[1536,640]{1,0:T(8,128)}) %all-reduce.22.cloned.1.call-update) | async-done | bytes 3932176 | tf_op jit(solution)/shard_map/psum | solution.py:185
  375.6 100.0 %all-reduce.24.cloned.1.call-done = f32[1536,640]{1,0:T(8,128)} async-done(((f32[1536,640]{1,0:T(8,128)}), f32[1536,640]{1,0:T(8,128)}) %all-reduce.24.cloned.1.call-update) | async-done | bytes 3932176 | tf_op jit(solution)/shard_map/psum | solution.py:200
  499.8 116.4 %while.30 = (s32[]{:T(128)}, f32[1536,256]{1,0:T(8,128)}, f32[1536,256]{1,0:T(8,128)S(1)}, f32[3,512,2,256]{3,1,2,0:T(8,128)}, s32[3]{0:T(128)S(1)}, /*index=5*/...) while((s32[]{:T(128)}, f32[1536,256]{1,0:T(8,128)}, ...), condition=%wide.region_21.22_spmd.clone.clone, body=%wide.region_19.21_spmd.clone.sunk.clone | while | flops 4054849536 | bytes 115111200 | solution.py:246
  515.6 12.1 fusion.188
  527.7 10.6 fusion.190
  554.1 12.5 fusion.188
  593.0 12.5 fusion.188
  605.5 10.7 fusion.190
  632.9 22.3 %multiply_reduce_fusion.9 = (f32[256]{0:T(256)S(1)}, f32[3,512,2]{2,1,0:T(8,128)S(1)}) fusion(f32[3,512,2,256]{3,2,1,0:T(2,128)S(1)} %copy-done.14, f32[3,512,2]{2,1,0:T(8,128)S(1)} %bitcast.271, f32[256]{0:T(256)S(1)} %broadcast_add_fusion.6, f32[3,512,2,128]{3,2,1,0:T(2,128)S(1)} %copy.137, f32[3,512,2,128]{3,2,1,0:T(2,128)S(1)} %copy.136, ...), kind=kLoop, calls=%fused_computation.124 | loop fusion | flops 7074560 | bytes 11036672 | tf_op jit(solution)/shard_map/reduce_sum | solution.py:60
  696.4 49.6 %reduce-scatter.6.cloned.1.call-done = f32[40,512]{1,0:T(8,128)} async-done(((f32[640,512]{1,0:T(8,128)}), f32[40,512]{1,0:T(8,128)}) %reduce-scatter.6.cloned.1.call-update) | async-done | bytes 81936 | tf_op jit(solution)/shard_map/reduce_scatter | solution.py:286
  746.1 67.4 %reduce-scatter.14.cloned.1.call-done = f32[64,640]{1,0:T(8,128)} async-done(((f32[1024,640]{1,0:T(8,128)}), f32[64,640]{1,0:T(8,128)}) %reduce-scatter.14.cloned.1.call-update) | async-done | bytes 163856 | tf_op jit(solution)/shard_map/reduce_scatter | solution.py:290
  813.6 67.7 %reduce-scatter.12.cloned.1.call-done = f32[40,1024]{1,0:T(8,128)} async-done(((f32[640,1024]{1,0:T(8,128)}), f32[40,1024]{1,0:T(8,128)}) %reduce-scatter.12.cloned.1.call-update) | async-done | bytes 163856 | tf_op jit(solution)/shard_map/reduce_scatter | solution.py:289
  881.3 67.6 %reduce-scatter.10.cloned.1.call-done = f32[40,1024]{1,0:T(8,128)} async-done(((f32[640,1024]{1,0:T(8,128)}), f32[40,1024]{1,0:T(8,128)}) %reduce-scatter.10.cloned.1.call-update) | async-done | bytes 163856 | tf_op jit(solution)/shard_map/reduce_scatter | solution.py:288
  960.6 28.7 %all-gather.8.cloned.1.call-done = f32[512,640]{1,0:T(8,128)} async-done(((f32[32,640]{1,0:T(8,128)}), f32[512,640]{1,0:T(8,128)}) %all-gather.8.cloned.1.call-update) | async-done | bytes 1310736 | tf_op jit(solution)/shard_map/all_gather | solution.py:299
  989.4 40.0 %all-gather.6.cloned.1.call-done = f32[640,512]{1,0:T(8,128)} async-done(((f32[40,512]{1,0:T(8,128)}), f32[640,512]{1,0:T(8,128)}) %all-gather.6.cloned.1.call-update) | async-done | bytes 1310736 | tf_op jit(solution)/shard_map/all_gather | solution.py:298
  1029.4 44.6 %all-gather.14.cloned.1.call-done = f32[1024,640]{1,0:T(8,128)} async-done(((f32[64,640]{1,0:T(8,128)}), f32[1024,640]{1,0:T(8,128)}) %all-gather.14.cloned.1.call-update) | async-done | bytes 2621456 | tf_op jit(solution)/shard_map/all_gather | solution.py:302
  1074.0 44.3 %all-gather.12.cloned.1.call-done = f32[640,1024]{1,0:T(8,128)} async-done(((f32[40,1024]{1,0:T(8,128)}), f32[640,1024]{1,0:T(8,128)}) %all-gather.12.cloned.1.call-update) | async-done | bytes 2621456 | tf_op jit(solution)/shard_map/all_gather | solution.py:301
  1118.3 44.4 %all-gather.10.cloned.1.call-done = f32[640,1024]{1,0:T(8,128)} async-done(((f32[40,1024]{1,0:T(8,128)}), f32[640,1024]{1,0:T(8,128)}) %all-gather.10.cloned.1.call-update) | async-done | bytes 2621456 | tf_op jit(solution)/shard_map/all_gather | solution.py:300
  1162.7 172.9 %all-reduce.28.cloned.1.call-done = (f32[1536,640]{1,0:T(8,128)}, f32[1536,256]{0,1:T(8,128)}, f32[1536,256]{1,0:T(8,128)}) async-done(((f32[1536,640]{1,0:T(8,128)}, f32[1536,256]{0,1:T(8,128)}, f32[1536,256]{1,0:T(8,128)}), (f32[1536,640]{1,0:T(8,128)}, f32[1536,256]{0,1:T(8,128)}, f32[1536,256]{1,0:T(8,128)})) %all-reduce.28.cloned.1.call-update) | async-done | bytes 7077904 | tf_op jit(solution)/shard_map/psum | solution.py:261
  1370.8 61.2 %all-reduce.11 = (f32[640]{0:T(1024)S(1)}, f32[256]{0:T(256)S(1)}, f32[640]{0:T(1024)S(1)}, f32[640]{0:T(1024)S(1)}, f32[640]{0:T(1024)S(1)}) all-reduce(f32[640]{0:T(1024)S(1)} %get-tuple-element.261, f32[256]{0:T(256)S(1)} %get-tuple-element.257, ...), channel_id=7, replica_groups=mesh['dp'=16,'tensor'=2] {'dp'}, use_global_device_ids=true, to_apply=%region_36.37.clone | all-reduce | flops 2816 | bytes 22528
  1437.9 58.1 %all-reduce.10 = (f32[640]{0:T(1024)}, f32[256]{0:T(256)}, f32[256]{0:T(256)}, f32[640]{0:T(1024)}, f32[640]{0:T(1024)}, /*index=5*/f32[640]{0:T(1024)}) all-reduce(f32[640]{0:T(1024)S(1)} %dynamic-slice_dynamic-update-slice_fusion.3, f32[256]{0:T(256)S(1)} %dynamic-update-slice.1, ...), channel_id=1, replica_groups=mesh['dp'=16,'tensor'=2] {'dp'}, use_global_device_ids=true, to_apply=%add | all-reduce | flops 3072 | bytes 24576
  1501.2 26.2 %all-reduce.26.cloned.1.call-done = (f32[640,256]{1,0:T(8,128)}, f32[640,256]{1,0:T(8,128)}) async-done(((f32[640,256]{1,0:T(8,128)}, f32[640,256]{1,0:T(8,128)}), (f32[640,256]{1,0:T(8,128)}, f32[640,256]{1,0:T(8,128)})) %all-reduce.26.cloned.1.call-update) | async-done | bytes 1310736 | tf_op jit(solution)/shard_map/psum | solution.py:278
  (391 shorter events, 356.4 us)
Async XLA Ops:
  7.2 232.4 %copy-start = (bf16[1024,640]{1,0:T(8,128)(2,1)S(1)}, bf16[1024,640]{1,0:T(8,128)(2,1)}, u32[]{:S(2)}) copy-start(bf16[1024,640]{1,0:T(8,128)(2,1)} %param.28) | copy-start | bytes 3932164
  7.2 215.1 %all-reduce.20.cloned.1.call-start = ((), (), s32[]{:S(2)}) async-start(), calls=%async_computation.5 | async-start | bytes 7864320 | tf_op jit(solution)/shard_map/psum | solution.py:176
  10.7 27.1 %copy-start.55 = (f32[640]{0:T(1024)}, f32[640]{0:T(1024)S(1)}, u32[]{:S(2)}) copy-start(f32[640]{0:T(1024)S(1)} %broadcast_add_fusion.4) | copy-start | bytes 7684
  12.7 25.1 %copy-start.53 = (f32[1536]{0:T(1024)}, f32[1536]{0:T(1024)S(1)}, u32[]{:S(2)}) copy-start(f32[1536]{0:T(1024)S(1)} %add_rsqrt_fusion.5) | copy-start | bytes 18436
  116.6 230.7 %all-reduce.22.cloned.1.call-start = ((), (), s32[]{:S(2)}) async-start(), calls=%async_computation.6 | async-start | bytes 7864320 | tf_op jit(solution)/shard_map/psum | solution.py:185
  244.2 105.7 %copy-start.21 = (bf16[1536,640]{1,0:T(8,128)(2,1)S(1)}, bf16[1536,640]{1,0:T(8,128)(2,1)}, u32[]{:S(2)}) copy-start(bf16[1536,640]{1,0:T(8,128)(2,1)} %param.35) | copy-start | bytes 5898244
  244.2 231.3 %all-reduce.24.cloned.1.call-start = ((), (), s32[]{:S(2)}) async-start(), calls=%async_computation.7 | async-start | bytes 7864320 | tf_op jit(solution)/shard_map/psum | solution.py:200
  372.5 323.2 %reduce-scatter.8.cloned.1.call-start = ((), (), s32[]{:S(2)}) async-start(), calls=%async_computation.10 | async-start | bytes 1392640 | tf_op jit(solution)/shard_map/reduce_scatter | solution.py:287
  554.1 12.5 copy-start.40
  593.0 12.5 copy-start.40
  625.9 120.1 %reduce-scatter.6.cloned.1.call-start = ((), (), s32[]{:S(2)}) async-start(), calls=%async_computation.8 | async-start | bytes 1392640 | tf_op jit(solution)/shard_map/reduce_scatter | solution.py:286
  676.1 137.4 %reduce-scatter.14.cloned.1.call-start = ((), (), s32[]{:S(2)}) async-start(), calls=%async_computation.16 | async-start | bytes 2785280 | tf_op jit(solution)/shard_map/reduce_scatter | solution.py:290
  683.0 198.2 %reduce-scatter.12.cloned.1.call-start = ((), (), s32[]{:S(2)}) async-start(), calls=%async_computation.14 | async-start | bytes 2785280 | tf_op jit(solution)/shard_map/reduce_scatter | solution.py:289
  689.3 259.6 %reduce-scatter.10.cloned.1.call-start = ((), (), s32[]{:S(2)}) async-start(), calls=%async_computation.12 | async-start | bytes 2785280 | tf_op jit(solution)/shard_map/reduce_scatter | solution.py:288
  695.6 256.4 %copy-start.45 = (bf16[640,512]{1,0:T(8,128)(2,1)S(1)}, bf16[640,512]{1,0:T(8,128)(2,1)}, u32[]{:S(2)}) copy-start(bf16[640,512]{1,0:T(8,128)(2,1)} %param.22) | copy-start | bytes 1966084
  695.6 293.7 %all-gather.8.cloned.1.call-start = ((), (), s32[]{:S(2)}) async-start(), calls=%async_computation.11 | async-start | bytes 1392640 | tf_op jit(solution)/shard_map/all_gather | solution.py:299
  696.4 333.0 %all-gather.6.cloned.1.call-start = ((), (), s32[]{:S(2)}) async-start(), calls=%async_computation.9 | async-start | bytes 1392640 | tf_op jit(solution)/shard_map/all_gather | solution.py:298
  746.0 328.0 %all-gather.14.cloned.1.call-start = ((), (), s32[]{:S(2)}) async-start(), calls=%async_computation.17 | async-start | bytes 2785280 | tf_op jit(solution)/shard_map/all_gather | solution.py:302
  813.5 304.8 %all-gather.12.cloned.1.call-start = ((), (), s32[]{:S(2)}) async-start(), calls=%async_computation.15 | async-start | bytes 2785280 | tf_op jit(solution)/shard_map/all_gather | solution.py:301
  881.2 281.5 %all-gather.10.cloned.1.call-start = ((), (), s32[]{:S(2)}) async-start(), calls=%async_computation.13 | async-start | bytes 2785280 | tf_op jit(solution)/shard_map/all_gather | solution.py:300
  949.0 386.6 %all-reduce.28.cloned.1.call-start = ((), (), s32[]{:S(2)}) async-start(), calls=%async_computation.19 | async-start | bytes 14155776 | tf_op jit(solution)/shard_map/psum | solution.py:261
  956.8 378.8 %copy-start.26 = (f32[1536,128]{0,1:T(8,128)S(1)}, f32[1536,128]{0,1:T(8,128)}, u32[]{:S(2)}) copy-start(f32[1536,128]{0,1:T(8,128)} %copy-done.25) | copy-start | bytes 2359300
  956.8 570.6 %all-reduce.26.cloned.1.call-start = ((), (), s32[]{:S(2)}) async-start(), calls=%async_computation.18 | async-start | bytes 2621440 | tf_op jit(solution)/shard_map/psum | solution.py:278
  1501.2 31.7 %copy-start.39 = (f32[512,640]{1,0:T(8,128)S(1)}, f32[512,640]{1,0:T(8,128)}, u32[]{:S(2)}) copy-start(f32[512,640]{1,0:T(8,128)} %all-gather.8.cloned.1.call-done) | copy-start | bytes 3932164
  (82 other events, 326.1 us)
Sparse Core Ops, SparseCore 0:
  116.7 105.5 all-reduce.19
  244.3 102.8 all-reduce.21
  372.6 102.8 all-reduce.23
  626.0 58.4 reduce-scatter.7
  688.5 57.4 reduce-scatter.5
  750.6 62.8 reduce-scatter.13
  818.3 62.8 reduce-scatter.11
  886.0 62.8 reduce-scatter.9
  951.5 37.8 all-gather.7
  991.7 37.6 all-gather.5
  1031.9 42.0 all-gather.13
  1076.4 41.8 all-gather.11
  1120.8 41.8 all-gather.9
  1166.0 169.5 all-reduce.27
  1437.1 90.2 all-reduce.25
where the time goes:
time: 1550 us
  waiting for transfers between devices  962 us (62%)
  matrix products  203 us (13%)
  other arithmetic  126 us (8%)
  blocking collectives  124 us (8%)
  local copies, waits for them, and re-layouts  101 us (7%)
  between operations  17.6 us (1%)
    psum x1, waiting for transfers between devices, local(): lax.psum((grad_keys_part, grad_values_part, right_dot(grad_query_low, w_q...  173 us
    unnamed x2, blocking collectives  119 us
    psum x1, waiting for transfers between devices, local(): lax.psum(jnp.dot(mixed_heads, w_output, preferred_element_type=jnp.float3...  105 us
    psum x1, waiting for transfers between devices, local(): lax.psum(jnp.dot(hidden, w_down, preferred_element_type=jnp.float32), 'te...  102 us
    psum x1, waiting for transfers between devices, local(): lax.psum(right_dot(grad_gate_low, w_gate) + right_dot(grad_up_low, w_up),...  100 us
    reduce_scatter x1, waiting for transfers between devices, local(): lax.psum_scatter(grad_up, 'dp', scatter_dimension=0, tiled=True)  67.7 us
    reduce_scatter x1, waiting for transfers between devices, local(): lax.psum_scatter(grad_gate, 'dp', scatter_dimension=0, tiled=True)  67.6 us
    reduce_scatter x1, waiting for transfers between devices, local(): lax.psum_scatter(grad_down, 'dp', scatter_dimension=0, tiled=True)  67.4 us
  transfers between devices with their start and end apart: 15, of which 14 were waited for; matrix products, arithmetic and copies ran while one was open for 5% of the time, Pallas kernels for 0%

commit v1 on v0

--- a/solution.py
+++ b/solution.py
@@ -6,6 +6,10 @@
 HD = 256
 EPS = 1e-06
 THETA = 1000000.0
+
+
+def derive_edge(load, mesh_ax):
+    return lax.all_gather(load, mesh_ax).sum(axis=0)
 
 
 def layout(lengths, holder, device, tok_rows):
@@ -197,7 +201,7 @@
     grad_up_low = (grad_hidden * activation).astype(jnp.bfloat16)
     grad_gate = left_dot(normed2_low, grad_gate_low)
     grad_up = left_dot(normed2_low, grad_up_low)
-    grad_normed2 = lax.psum(
+    grad_normed2 = derive_edge(
         right_dot(grad_gate_low, w_gate) + right_dot(grad_up_low, w_up), "tensor"
     )
     grad_pre_part, grad_pre_ffn = norm_backward(

time: 1550 us -> 1400 us (0.903)
  waiting for transfers between devices: 962 us -> 811 us
    psum x1 -> x0, waiting for transfers between devices: 100 us -> none  [local(): lax.psum(right_dot(grad_gate_low, w_gate) + right_dot(grad_up_low, w_up),...]
    all_gather x0 -> x1, waiting for transfers between devices: none -> 75 us  [derive_edge(): return lax.all_gather(load, mesh_ax).sum(axis=0)]
    reduce_scatter x1, waiting for transfers between devices: 67.7 us -> 0.02 us  [local(): lax.psum_scatter(grad_up, 'dp', scatter_dimension=0, tiled=True)]
    reduce_scatter x1, waiting for transfers between devices: 67.4 us -> 0.02 us  [local(): lax.psum_scatter(grad_down, 'dp', scatter_dimension=0, tiled=True)]
    reduce_scatter x1, waiting for transfers between devices: 67.6 us -> 3.64 us  [local(): lax.psum_scatter(grad_gate, 'dp', scatter_dimension=0, tiled=True)]
    reduce_scatter x1, waiting for transfers between devices: 0.02 us -> 61.6 us  [local(): lax.psum_scatter(grad_output, 'dp', scatter_dimension=0, tiled=True)]
    unnamed x170 -> x166, local copies, waits for them, and re-layouts: 37.3 us -> 36.8 us
  transfers between devices with their start and end apart: 15 -> 15, of which waited for: 14 -> 13; matrix products, arithmetic and copies ran while one was open for 5% -> 16% of each run, Pallas kernels for 0% -> 0%
where the time goes in v1:
time: 1400 us; the launch traced here: 1390 us
  waiting for transfers between devices  811 us (58%)
  matrix products  204 us (15%)
  blocking collectives  124 us (9%)
  other arithmetic  120 us (9%)
  local copies, waits for them, and re-layouts  104 us (7%)
  between operations  17.7 us (1%)
    psum x1, waiting for transfers between devices, local(): lax.psum((grad_keys_part, grad_values_part, right_dot(grad_query_low, w_q...  173 us
    unnamed x2, blocking collectives  119 us
    psum x1, waiting for transfers between devices, local(): lax.psum(jnp.dot(mixed_heads, w_output, preferred_element_type=jnp.float3...  105 us
    psum x1, waiting for transfers between devices, local(): lax.psum(jnp.dot(hidden, w_down, preferred_element_type=jnp.float32), 'te...  102 us
    all_gather x1, waiting for transfers between devices, derive_edge(): return lax.all_gather(load, mesh_ax).sum(axis=0)  75 us
    reduce_scatter x1, waiting for transfers between devices, local(): lax.psum_scatter(grad_query, 'dp', scatter_dimension=0, tiled=True)  62 us
    reduce_scatter x1, waiting for transfers between devices, local(): lax.psum_scatter(grad_output, 'dp', scatter_dimension=0, tiled=True)  61.6 us
    all_gather x1, waiting for transfers between devices, local(): lax.all_gather(all_summed[2], 'dp', axis=0, tiled=True)  44.2 us
  transfers between devices with their start and end apart: 15, of which 13 were waited for; matrix products, arithmetic and copies ran while one was open for 16% of the time, Pallas kernels for 0%

profile of v1, /device:TPU:0, one launch (start us, length us, event | category | flops | bytes accessed | tf_op | source)
XLA Modules:
  0.0 1393.5 jit_solution(11422838358714941327)
XLA Ops:
  69.3 39.2 %while.29 = (s32[]{:T(128)}, bf16[3,512,2,256]{3,1,2,0:T(8,128)(2,1)}, f32[3,2,512]{2,1,0:T(2,128)S(1)}, s32[3]{0:T(128)S(1)}, s32[1536]{0:T(1024)S(1)}, /*index...) while((s32[]{:T(128)}, ...), condition=%wide.region_9.10_spmd.clone, body=%wide.region_6.9_spmd.sunk.clone | while | flops 1634205696 | bytes 40944880 | solution.py:178
  117.2 105.1 %all-reduce.19.cloned.1.call-done = f32[1536,640]{1,0:T(8,128)} async-done(((f32[1536,640]{1,0:T(8,128)}), f32[1536,640]{1,0:T(8,128)}) %all-reduce.19.cloned.1.call-update) | async-done | bytes 3932176 | tf_op jit(solution)/shard_map/psum | solution.py:180
  244.7 102.4 %all-reduce.21.cloned.1.call-done = f32[1536,640]{1,0:T(8,128)} async-done(((f32[1536,640]{1,0:T(8,128)}), f32[1536,640]{1,0:T(8,128)}) %all-reduce.21.cloned.1.call-update) | async-done | bytes 3932176 | tf_op jit(solution)/shard_map/psum | solution.py:189
  395.7 75.0 %all-gather.18.cloned.1.call-done = f32[3072,640]{1,0:T(8,128)} async-done(((f32[1536,640]{1,0:T(8,128)}), f32[3072,640]{1,0:T(8,128)}) %all-gather.18.cloned.1.call-update) | async-done | bytes 7864336 | tf_op jit(solution)/shard_map/all_gather | solution.py:12
  496.9 118.3 %while.30 = (s32[]{:T(128)}, f32[1536,256]{1,0:T(8,128)}, f32[1536,256]{1,0:T(8,128)S(1)}, f32[3,512,2,256]{3,1,2,0:T(8,128)}, s32[3]{0:T(128)S(1)}, /*index=5*/...) while((s32[]{:T(128)}, f32[1536,256]{1,0:T(8,128)}, ...), condition=%wide.region_21.22_spmd.clone.clone, body=%wide.region_19.21_spmd.clone.sunk.clone | while | flops 4054849536 | bytes 115111200 | solution.py:250
  513.1 12.3 fusion.188
  525.3 10.7 fusion.190
  551.7 13.5 fusion.188
  565.2 11.0 fusion.190
  592.0 12.6 fusion.188
  604.6 10.7 fusion.190
  635.8 10.9 multiply_reduce_fusion.9
  672.8 61.6 %reduce-scatter.8.cloned.1.call-done = f32[32,640]{1,0:T(8,128)} async-done(((f32[512,640]{1,0:T(8,128)}), f32[32,640]{1,0:T(8,128)}) %reduce-scatter.8.cloned.1.call-update) | async-done | bytes 81936 | tf_op jit(solution)/shard_map/reduce_scatter | solution.py:291
  734.5 62.0 %reduce-scatter.6.cloned.1.call-done = f32[40,512]{1,0:T(8,128)} async-done(((f32[640,512]{1,0:T(8,128)}), f32[40,512]{1,0:T(8,128)}) %reduce-scatter.6.cloned.1.call-update) | async-done | bytes 81936 | tf_op jit(solution)/shard_map/reduce_scatter | solution.py:290
  808.2 32.7 %all-gather.16.cloned.1.call-done = f32[1024,640]{1,0:T(8,128)} async-done(((f32[64,640]{1,0:T(8,128)}), f32[1024,640]{1,0:T(8,128)}) %all-gather.16.cloned.1.call-update) | async-done | bytes 2621456 | tf_op jit(solution)/shard_map/all_gather | solution.py:306
  840.9 44.0 %all-gather.14.cloned.1.call-done = f32[640,1024]{1,0:T(8,128)} async-done(((f32[40,1024]{1,0:T(8,128)}), f32[640,1024]{1,0:T(8,128)}) %all-gather.14.cloned.1.call-update) | async-done | bytes 2621456 | tf_op jit(solution)/shard_map/all_gather | solution.py:305
  884.9 44.2 %all-gather.12.cloned.1.call-done = f32[640,1024]{1,0:T(8,128)} async-done(((f32[40,1024]{1,0:T(8,128)}), f32[640,1024]{1,0:T(8,128)}) %all-gather.12.cloned.1.call-update) | async-done | bytes 2621456 | tf_op jit(solution)/shard_map/all_gather | solution.py:304
  929.1 39.6 %all-gather.10.cloned.1.call-done = f32[512,640]{1,0:T(8,128)} async-done(((f32[32,640]{1,0:T(8,128)}), f32[512,640]{1,0:T(8,128)}) %all-gather.10.cloned.1.call-update) | async-done | bytes 1310736 | tf_op jit(solution)/shard_map/all_gather | solution.py:303
  968.7 39.9 %all-gather.8.cloned.1.call-done = f32[640,512]{1,0:T(8,128)} async-done(((f32[40,512]{1,0:T(8,128)}), f32[640,512]{1,0:T(8,128)}) %all-gather.8.cloned.1.call-update) | async-done | bytes 1310736 | tf_op jit(solution)/shard_map/all_gather | solution.py:302
  1008.7 172.8 %all-reduce.25.cloned.1.call-done = (f32[1536,640]{1,0:T(8,128)}, f32[1536,256]{0,1:T(8,128)}, f32[1536,256]{1,0:T(8,128)}) async-done(((f32[1536,640]{1,0:T(8,128)}, f32[1536,256]{0,1:T(8,128)}, f32[1536,256]{1,0:T(8,128)}), (f32[1536,640]{1,0:T(8,128)}, f32[1536,256]{0,1:T(8,128)}, f32[1536,256]{1,0:T(8,128)})) %all-reduce.25.cloned.1.call-update) | async-done | bytes 7077904 | tf_op jit(solution)/shard_map/psum | solution.py:265
  1207.8 8.9 fusion.65
  1216.6 61.2 %all-reduce.11 = (f32[640]{0:T(1024)S(1)}, f32[256]{0:T(256)S(1)}, f32[640]{0:T(1024)S(1)}, f32[640]{0:T(1024)S(1)}, f32[640]{0:T(1024)S(1)}) all-reduce(f32[640]{0:T(1024)S(1)} %get-tuple-element.261, f32[256]{0:T(256)S(1)} %get-tuple-element.257, ...), channel_id=8, replica_groups=mesh['dp'=16,'tensor'=2] {'dp'}, use_global_device_ids=true, to_apply=%region_36.37.clone | all-reduce | flops 2816 | bytes 22528
  1283.7 58.3 %all-reduce.10 = (f32[640]{0:T(1024)}, f32[256]{0:T(256)}, f32[256]{0:T(256)}, f32[640]{0:T(1024)}, f32[640]{0:T(1024)}, /*index=5*/f32[640]{0:T(1024)}) all-reduce(f32[640]{0:T(1024)S(1)} %dynamic-slice_dynamic-update-slice_fusion.3, f32[256]{0:T(256)S(1)} %dynamic-update-slice.1, ...), channel_id=1, replica_groups=mesh['dp'=16,'tensor'=2] {'dp'}, use_global_device_ids=true, to_apply=%add | all-reduce | flops 3072 | bytes 24576
  1347.1 26.1 %all-reduce.23.cloned.1.call-done = (f32[640,256]{1,0:T(8,128)}, f32[640,256]{1,0:T(8,128)}) async-done(((f32[640,256]{1,0:T(8,128)}, f32[640,256]{1,0:T(8,128)}), (f32[640,256]{1,0:T(8,128)}, f32[640,256]{1,0:T(8,128)})) %all-reduce.23.cloned.1.call-update) | async-done | bytes 1310736 | tf_op jit(solution)/shard_map/psum | solution.py:282
  (388 shorter events, 347.6 us)
Async XLA Ops:
  7.2 232.3 %copy-start = (bf16[1024,640]{1,0:T(8,128)(2,1)S(1)}, bf16[1024,640]{1,0:T(8,128)(2,1)}, u32[]{:S(2)}) copy-start(bf16[1024,640]{1,0:T(8,128)(2,1)} %param.28) | copy-start | bytes 3932164
  7.2 215.0 %all-reduce.19.cloned.1.call-start = ((), (), s32[]{:S(2)}) async-start(), calls=%async_computation.5 | async-start | bytes 7864320 | tf_op jit(solution)/shard_map/psum | solution.py:180
  10.7 27.0 %copy-start.54 = (f32[640]{0:T(1024)}, f32[640]{0:T(1024)S(1)}, u32[]{:S(2)}) copy-start(f32[640]{0:T(1024)S(1)} %broadcast_add_fusion.4) | copy-start | bytes 7684
  12.7 24.9 %copy-start.52 = (f32[1536]{0:T(1024)}, f32[1536]{0:T(1024)S(1)}, u32[]{:S(2)}) copy-start(f32[1536]{0:T(1024)S(1)} %add_rsqrt_fusion.5) | copy-start | bytes 18436
  116.5 230.7 %all-reduce.21.cloned.1.call-start = ((), (), s32[]{:S(2)}) async-start(), calls=%async_computation.6 | async-start | bytes 7864320 | tf_op jit(solution)/shard_map/psum | solution.py:189
  244.1 105.7 %copy-start.19 = (bf16[1536,640]{1,0:T(8,128)(2,1)S(1)}, bf16[1536,640]{1,0:T(8,128)(2,1)}, u32[]{:S(2)}) copy-start(bf16[1536,640]{1,0:T(8,128)(2,1)} %param.35) | copy-start | bytes 5898244
  244.1 226.5 %all-gather.18.cloned.1.call-start = ((), (), s32[]{:S(2)}) async-start(), calls=%async_computation.17 | async-start | bytes 11796480 | tf_op jit(solution)/shard_map/all_gather | solution.py:12
  372.4 295.5 %reduce-scatter.14.cloned.1.call-start = ((), (), s32[]{:S(2)}) async-start(), calls=%async_computation.15 | async-start | bytes 2785280 | tf_op jit(solution)/shard_map/reduce_scatter | solution.py:294
  379.2 289.3 %reduce-scatter.12.cloned.1.call-start = ((), (), s32[]{:S(2)}) async-start(), calls=%async_computation.13 | async-start | bytes 2785280 | tf_op jit(solution)/shard_map/reduce_scatter | solution.py:293
  385.6 287.1 %reduce-scatter.10.cloned.1.call-start = ((), (), s32[]{:S(2)}) async-start(), calls=%async_computation.11 | async-start | bytes 2785280 | tf_op jit(solution)/shard_map/reduce_scatter | solution.py:292
  395.6 338.9 %reduce-scatter.8.cloned.1.call-start = ((), (), s32[]{:S(2)}) async-start(), calls=%async_computation.9 | async-start | bytes 1392640 | tf_op jit(solution)/shard_map/reduce_scatter | solution.py:291
  551.7 13.5 copy-start.39
  592.0 12.6 copy-start.39
  635.7 160.9 %reduce-scatter.6.cloned.1.call-start = ((), (), s32[]{:S(2)}) async-start(), calls=%async_computation.7 | async-start | bytes 1392640 | tf_op jit(solution)/shard_map/reduce_scatter | solution.py:290
  667.7 131.9 %copy-start.44 = (bf16[640,512]{1,0:T(8,128)(2,1)S(1)}, bf16[640,512]{1,0:T(8,128)(2,1)}, u32[]{:S(2)}) copy-start(bf16[640,512]{1,0:T(8,128)(2,1)} %param.22) | copy-start | bytes 1966084
  667.8 173.1 %all-gather.16.cloned.1.call-start = ((), (), s32[]{:S(2)}) async-start(), calls=%async_computation.16 | async-start | bytes 2785280 | tf_op jit(solution)/shard_map/all_gather | solution.py:306
  668.5 216.4 %all-gather.14.cloned.1.call-start = ((), (), s32[]{:S(2)}) async-start(), calls=%async_computation.14 | async-start | bytes 2785280 | tf_op jit(solution)/shard_map/all_gather | solution.py:305
  669.1 260.0 %all-gather.12.cloned.1.call-start = ((), (), s32[]{:S(2)}) async-start(), calls=%async_computation.12 | async-start | bytes 2785280 | tf_op jit(solution)/shard_map/all_gather | solution.py:304
  672.8 296.0 %all-gather.10.cloned.1.call-start = ((), (), s32[]{:S(2)}) async-start(), calls=%async_computation.10 | async-start | bytes 1392640 | tf_op jit(solution)/shard_map/all_gather | solution.py:303
  734.5 274.2 %all-gather.8.cloned.1.call-start = ((), (), s32[]{:S(2)}) async-start(), calls=%async_computation.8 | async-start | bytes 1392640 | tf_op jit(solution)/shard_map/all_gather | solution.py:302
  796.6 384.9 %all-reduce.25.cloned.1.call-start = ((), (), s32[]{:S(2)}) async-start(), calls=%async_computation.19 | async-start | bytes 14155776 | tf_op jit(solution)/shard_map/psum | solution.py:265
  804.4 377.1 %copy-start.23 = (f32[1536,128]{0,1:T(8,128)S(1)}, f32[1536,128]{0,1:T(8,128)}, u32[]{:S(2)}) copy-start(f32[1536,128]{0,1:T(8,128)} %copy-done.22) | copy-start | bytes 2359300
  804.4 568.8 %all-reduce.23.cloned.1.call-start = ((), (), s32[]{:S(2)}) async-start(), calls=%async_computation.18 | async-start | bytes 2621440 | tf_op jit(solution)/shard_map/psum | solution.py:282
  1347.1 31.6 %copy-start.38 = (f32[512,640]{1,0:T(8,128)S(1)}, f32[512,640]{1,0:T(8,128)}, u32[]{:S(2)}) copy-start(f32[512,640]{1,0:T(8,128)} %all-gather.10.cloned.1.call-done) | copy-start | bytes 3932164
  (80 other events, 323.9 us)
Sparse Core Ops, SparseCore 0:
  116.6 105.6 all-reduce.18
  244.2 102.8 all-reduce.20
  372.5 98.0 all-gather.17
  474.8 63.8 reduce-scatter.13
  542.9 62.7 reduce-scatter.11
  609.9 62.8 reduce-scatter.9
  677.0 57.4 reduce-scatter.7
  739.1 57.4 reduce-scatter.5
  798.8 41.9 all-gather.15
  843.0 41.8 all-gather.13
  887.2 41.8 all-gather.11
  931.2 37.4 all-gather.9
  971.0 37.6 all-gather.7
  1011.7 169.7 all-reduce.24
  1282.9 90.2 all-reduce.22
